TPU v7x, 32 devices: a whole 2x2x4 slice. The times are simulated.
32 devices in a mesh: grp: 2 (over y), req: 4 (over z), tp: 4 (over x, core).
Axes of the slice: x: 2, y: 2, z: 4, core: 2. Of those that a mesh axis runs over, the one named last changes fastest.
Arguments:
- queries: bfloat16 [8, 256, 64, 128], P(('grp', 'req'), None, 'tp'), parts along dimension 0, may hold values from -200 to 200
- kv_new: bfloat16 [8, 256, 2, 8, 128], P(('grp', 'req'), None, None, 'tp'), parts along dimension 0, may hold values from -4 to 4
- kv_codes: bfloat16 [64, 2, 8, 128, 128], P(('grp', 'req'), None, 'tp'), parts along dimension 0, may hold values from -4 to 4
- kv_scale: bfloat16 [64, 2, 8, 128], P(('grp', 'req'), None, 'tp'), parts along dimension 0, may hold values from 0.5 to 2
- block_owner: int32 [8, 24], P('grp'), parts along dimension 0, may hold values from 0 to 3, as said below
- block_index: int32 [8, 24], P('grp'), parts along dimension 0, may hold values from 0 to 7
- prefix_blocks: int32 [8], P('grp'), parts along dimension 0, may hold values from 1 to 24, as said below
- state_owner: int32 [8], P('grp'), parts along dimension 0, may hold values from 0 to 3, as said below
- ssm_pool: float32 [8, 128, 64, 256], P(('grp', 'req'), 'tp'), parts along dimension 0, may hold values from -0.375 to 0.375
- conv_pool_x: bfloat16 [8, 3, 8192], P(('grp', 'req'), None, 'tp'), parts along dimension 0, may hold values from -4 to 4
- conv_pool_bc: bfloat16 [8, 3, 2, 2048], P(('grp', 'req'), None, None, 'tp'), parts along dimension 0, may hold values from -4 to 4
- x_in: bfloat16 [8, 256, 8192], P(('grp', 'req'), None, 'tp'), parts along dimension 0, may hold values from -5 to 5
- bc_in: bfloat16 [8, 256, 2, 2048], P(('grp', 'req'), None, None, 'tp'), parts along dimension 0, may hold values from -5 to 5
- z_in: bfloat16 [8, 256, 8192], P(('grp', 'req'), None, 'tp'), parts along dimension 0, may hold values from -5 to 5
- dt_raw: float32 [8, 256, 128], P(('grp', 'req'), None, 'tp'), parts along dimension 0, may hold values from -5 to 5
- dt_bias: float32 [128], P('tp'), may hold values from -4 to -2
- ssm_rate: float32 [128], P('tp'), may hold values from 0.03 to 1
- skip_gain: float32 [128], P('tp'), may hold values from 0.5 to 1.5
- conv_weight_x: bfloat16 [4, 8192], P(None, 'tp'), may hold values from -3 to 3
- conv_weight_bc: bfloat16 [4, 2, 2048], P(None, None, 'tp'), may hold values from -3 to 3
- conv_bias_x: bfloat16 [8192], P('tp'), may hold values from -2.5 to 2.5
- conv_bias_bc: bfloat16 [2, 2048], P(None, 'tp'), may hold values from -2.5 to 2.5
- norm_gain: bfloat16 [8192], P('tp'), may hold values from 0.099609375 to 1.8984375
Outputs:
- ssm_out: bfloat16 [8, 256, 8192], P(('grp', 'req'), None, 'tp'), parts along dimension 0
- attn_out: bfloat16 [8, 256, 64, 128], P(('grp', 'req'), None, 'tp'), parts along dimension 0
There are 2 independent parts, one for each index of `grp`. A program takes and returns all parts, laid end to end along the dimension named above; an argument that names none is the same for every part. Nothing has to cross between parts.
Inputs may be any that keep to these rules, and one draw needn't show every extreme that they name: `block_owner`: entries name devices along req. At most 6 of the 24 entries of one request name the same owner, and in every draw some owner is named exactly 6 times by every request. Only the first prefix_blocks[r] entries of request r's table belong to its prefix; the other entries are unused. `state_owner`: A permutation: each owner holds the cached states of exactly one request.
All inputs are finite; a program needn't handle non-finite values.
Results may differ from a plain program's by a relative error of at most 0.0073.
Values may be sent and summed in bfloat16 or wider, within the bound.
A program may use at most 64 MiB of HBM per device.

v0:
```python
import functools
import math

import jax
import jax.numpy as jnp
from jax import lax
from jax.experimental import pallas as pl
from jax.experimental.pallas import tpu as pltpu
from jax.sharding import PartitionSpec as P

F32 = jnp.float32
BF16 = jnp.bfloat16
VMEM_LIMIT = 48 * 1024 * 1024


def hadamard_signs(order_len):
    index_row = jnp.arange(order_len, dtype=jnp.int32)
    common_bits = jnp.bitwise_and(index_row[:, None], index_row[None, :])
    parity = jnp.zeros((order_len, order_len), jnp.int32)
    for shift_by in range(max(order_len.bit_length() - 1, 0)):
        parity = parity + jnp.bitwise_and(jnp.right_shift(common_bits, shift_by), 1)
    return jnp.where(parity % 2 == 0, 1.0, -1.0).astype(BF16)


def dequantize(block_codes, scales, sign_table):
    row_width = block_codes.shape[-1]
    rotated = jnp.dot(
        block_codes.reshape(-1, row_width), sign_table, preferred_element_type=F32
    )
    rotated = rotated.reshape(block_codes.shape)
    return (rotated * scales.astype(F32)[..., None] * (1.0 / math.sqrt(row_width))).astype(BF16)


def causal_conv(history, incoming, weight, bias_row):
    joined = jnp.concatenate([history, incoming], axis=0).astype(F32)
    length = incoming.shape[0]
    summed = jnp.broadcast_to(bias_row.astype(F32), incoming.shape)
    for offset in range(weight.shape[0]):
        summed = summed + weight[offset].astype(F32) * joined[offset : offset + length]
    return jax.nn.silu(summed).astype(BF16)


def ssm_before_state(conv_x, conv_b, conv_c, step_raw, dt_bias, ssm_rate, skip_gain, state_dim):
    length, heads_here = step_raw.shape
    head_dim = conv_x.shape[1] // heads_here
    groups = conv_b.shape[1] // state_dim
    per_group = heads_here // groups
    step_size = jax.nn.softplus(step_raw + dt_bias)
    cumulative = jnp.cumsum(-step_size * ssm_rate, axis=0)
    b_rows = conv_b.reshape(length, groups, state_dim)
    c_rows = conv_c.reshape(length, groups, state_dim)
    gram_rows = jnp.einsum("tgn,sgn->gts", c_rows, b_rows, preferred_element_type=F32)
    by_head = cumulative.T
    log_decay = by_head[:, :, None] - by_head[:, None, :]
    position = jnp.arange(length)
    lower_mask = position[None, :] <= position[:, None]
    decay_mat = jnp.exp(jnp.where(lower_mask[None], log_decay, -jnp.inf))
    mix_rows = (gram_rows[:, None] * decay_mat.reshape(groups, per_group, length, length)).astype(
        BF16
    )
    x_heads = conv_x.reshape(length, heads_here, head_dim).astype(F32)
    scaled_x = (x_heads * step_size[:, :, None]).astype(BF16)
    intra_term = jnp.einsum(
        "gkts,sgkp->tgkp",
        mix_rows,
        scaled_x.reshape(length, groups, per_group, head_dim),
        preferred_element_type=F32,
    ).reshape(length, heads_here * head_dim)
    near = intra_term + jnp.repeat(skip_gain, head_dim)[None, :] * conv_x.astype(F32)
    decay = jnp.repeat(jnp.exp(cumulative), head_dim, axis=1)
    return near, decay


def tail_kernel(c_ref, state_ref, near_ref, decay_ref, z_ref, gain_ref, out_ref):
    carried = lax.dot_general(
        c_ref[...], state_ref[...], (((1,), (1,)), ((), ())), preferred_element_type=F32
    )
    y_heads = near_ref[...] + carried * decay_ref[...]
    gate = z_ref[...].astype(F32)
    gated = y_heads * (gate / (1.0 + jnp.exp(-gate)))
    mean_square = jnp.mean(gated * gated, axis=1, keepdims=True)
    out_ref[...] = (
        gated * lax.rsqrt(mean_square + 1e-05) * gain_ref[...].astype(F32)
    ).astype(BF16)


def ssm_tail(c_rows, state, near, decay, gate_rows, norm_gain):
    length, width = gate_rows.shape
    state_dim = state.shape[1]
    groups = c_rows.shape[1] // state_dim
    span = width // groups
    wide = pl.BlockSpec((length, span), lambda g: (0, g))
    return pl.pallas_call(
        tail_kernel,
        grid=(groups,),
        out_shape=jax.ShapeDtypeStruct((length, width), BF16),
        in_specs=[
            pl.BlockSpec((length, state_dim), lambda g: (0, g)),
            pl.BlockSpec((span, state_dim), lambda g: (g, 0)),
            wide,
            wide,
            wide,
            pl.BlockSpec((1, span), lambda g: (0, g)),
        ],
        out_specs=wide,
        compiler_params=pltpu.CompilerParams(vmem_limit_bytes=VMEM_LIMIT),
        cost_estimate=pl.CostEstimate(
            flops=2 * length * width * state_dim,
            bytes_accessed=length * width * 12 + width * state_dim * 2,
            transcendentals=length * width,
        ),
    )(c_rows, state, near, decay, gate_rows, norm_gain.reshape(1, -1))


def attend_kernel(rows_ref, live_ref, q_ref, new_ref, pool_ref, out_ref, key_buf, val_buf):
    kv_here = new_ref.shape[1]
    length = new_ref.shape[2]
    width = new_ref.shape[3]
    block_len = pool_ref.shape[3]
    table_len = rows_ref.shape[0]
    old_len = table_len * block_len
    tile, heads_here, _ = q_ref.shape
    share = heads_here // kv_here
    step = pl.program_id(0)

    @pl.when(step == 0)
    def _():
        def gather(entry, carry):
            row = rows_ref[entry]
            is_live = (entry < live_ref[0]).astype(F32)
            spot = pl.ds(pl.multiple_of(entry * block_len, block_len), block_len)
            for head in range(kv_here):
                key_buf[head, spot, :] = pool_ref[row, 0, head]
                values = pool_ref[row, 1, head].astype(F32) * is_live
                val_buf[head, spot, 0:width] = values.astype(BF16)
                val_buf[head, spot, width : 2 * width] = jnp.full(
                    (block_len, width), is_live, F32
                ).astype(BF16)
            return carry

        lax.fori_loop(0, table_len, gather, 0)
        for head in range(kv_here):
            key_buf[head, old_len : old_len + length, :] = new_ref[0, head]
            val_buf[head, old_len : old_len + length, 0:width] = new_ref[1, head]
            val_buf[head, old_len : old_len + length, width : 2 * width] = jnp.ones(
                (length, width), BF16
            )

    to_exp2 = math.log2(math.e) / math.sqrt(width)
    all_q = q_ref[...].astype(F32)
    count = tile * share
    row_id = lax.broadcasted_iota(jnp.int32, (count, length), 0)
    column = lax.broadcasted_iota(jnp.int32, (count, length), 1)
    causal = column * share <= row_id + step * count
    parts = []
    for head in range(kv_here):
        head_q = all_q[:, head * share : (head + 1) * share, :].reshape(count, width).astype(BF16)
        contract = (((1,), (1,)), ((), ()))
        score_old = lax.dot_general(
            head_q, key_buf[head, 0:old_len, :], contract, preferred_element_type=F32
        )
        score_new = lax.dot_general(
            head_q,
            key_buf[head, old_len : old_len + length, :],
            contract,
            preferred_element_type=F32,
        )
        score_new = jnp.where(causal, score_new, -jnp.inf)
        row_max = jnp.maximum(
            jnp.max(score_old, axis=1, keepdims=True), jnp.max(score_new, axis=1, keepdims=True)
        )
        weight_old = jnp.exp2((score_old - row_max) * to_exp2).astype(BF16)
        weight_new = jnp.exp2((score_new - row_max) * to_exp2).astype(BF16)
        total = jnp.dot(weight_old, val_buf[head, 0:old_len, :], preferred_element_type=F32)
        total = total + jnp.dot(
            weight_new,
            val_buf[head, old_len : old_len + length, :],
            preferred_element_type=F32,
        )
        parts.append((total[:, 0:width] / total[:, width : 2 * width]).reshape(tile, share, width))
    out_ref[...] = jnp.concatenate(parts, axis=1).astype(BF16)


def attend(query_rows, new_rows, pool, rows, live):
    length, heads_here, width = query_rows.shape
    kv_here = new_rows.shape[1]
    table_len = rows.shape[0]
    keys = table_len * pool.shape[3] + length
    tile = 32
    whole = lambda i, *_: (0, 0, 0, 0)
    return pl.pallas_call(
        attend_kernel,
        grid_spec=pltpu.PrefetchScalarGridSpec(
            num_scalar_prefetch=2,
            grid=(length // tile,),
            in_specs=[
                pl.BlockSpec((tile, heads_here, width), lambda i, *_: (i, 0, 0)),
                pl.BlockSpec(new_rows.shape, whole),
                pl.BlockSpec(memory_space=pltpu.VMEM),
            ],
            out_specs=pl.BlockSpec((tile, heads_here, width), lambda i, *_: (i, 0, 0)),
            scratch_shapes=[
                pltpu.VMEM((kv_here, keys, width), BF16),
                pltpu.VMEM((kv_here, keys, 2 * width), BF16),
            ],
        ),
        out_shape=jax.ShapeDtypeStruct(query_rows.shape, BF16),
        compiler_params=pltpu.CompilerParams(vmem_limit_bytes=VMEM_LIMIT),
        cost_estimate=pl.CostEstimate(
            flops=8 * length * heads_here * keys * width,
            bytes_accessed=pool.size * 2 + 4 * query_rows.size,
            transcendentals=length * heads_here * keys,
        ),
    )(rows, live, query_rows, new_rows, pool)


def body(
    queries,
    kv_new,
    kv_codes,
    kv_scale,
    block_owner,
    block_index,
    prefix_blocks,
    state_owner,
    ssm_pool,
    conv_pool_x,
    conv_pool_bc,
    x_in,
    bc_in,
    z_in,
    dt_raw,
    dt_bias,
    ssm_rate,
    skip_gain,
    conv_weight_x,
    conv_weight_bc,
    conv_bias_x,
    conv_bias_bc,
    norm_gain,
):
    owners = lax.axis_size("req")
    my_index = lax.axis_index("req")
    held = kv_codes.shape[0]
    state_dim = ssm_pool.shape[3]

    own_blocks = dequantize(kv_codes, kv_scale, hadamard_signs(kv_codes.shape[-1]))
    pool = lax.all_gather(own_blocks, "req", axis=0, tiled=True)

    taps = conv_pool_x.shape[1]
    rows_x = conv_pool_x.shape[2]
    rows_bc = conv_pool_bc.shape[3]
    history = jnp.concatenate(
        [conv_pool_x[0], conv_pool_bc[0, :, 0], conv_pool_bc[0, :, 1]], axis=1
    )
    all_history = lax.all_gather(history, "req", axis=0)
    my_source = lax.dynamic_index_in_dim(state_owner, my_index, 0, keepdims=False)
    my_history = lax.dynamic_index_in_dim(all_history, my_source, 0, keepdims=False)

    state_rows = ssm_pool[0].reshape(-1, state_dim).astype(BF16)
    spread = lax.all_to_all(state_rows, "req", split_axis=0, concat_axis=0, tiled=True)
    chosen = jnp.take(
        spread.reshape(owners, -1, state_dim), state_owner, axis=0, mode="clip"
    ).reshape(-1, state_dim)
    state = lax.all_to_all(chosen, "req", split_axis=0, concat_axis=0, tiled=True)

    conv_x = causal_conv(my_history[:, :rows_x], x_in[0], conv_weight_x, conv_bias_x)
    conv_b = causal_conv(
        my_history[:, rows_x : rows_x + rows_bc],
        bc_in[0, :, 0],
        conv_weight_bc[:, 0],
        conv_bias_bc[0],
    )
    conv_c = causal_conv(
        my_history[:, rows_x + rows_bc :], bc_in[0, :, 1], conv_weight_bc[:, 1], conv_bias_bc[1]
    )
    near, decay = ssm_before_state(
        conv_x, conv_b, conv_c, dt_raw[0], dt_bias, ssm_rate, skip_gain, state_dim
    )

    live = lax.dynamic_slice_in_dim(prefix_blocks, my_index, 1, 0)
    table = block_owner * held + block_index
    my_table = lax.dynamic_index_in_dim(table, my_index, 0, keepdims=False)
    rows = jnp.where(jnp.arange(my_table.shape[0]) < live, my_table, my_table[0])
    new_rows = kv_new[0].transpose(1, 2, 0, 3)
    attended = attend(queries[0], new_rows, pool, rows, live)

    ssm_rows = ssm_tail(conv_c, state, near, decay, z_in[0], norm_gain)
    return (ssm_rows[None], attended[None])


def solution(mesh):
    placed = (
        P(("grp", "req"), None, "tp", None),
        P(("grp", "req"), None, None, "tp", None),
        P(("grp", "req"), None, "tp", None, None),
        P(("grp", "req"), None, "tp", None),
        P("grp", None),
        P("grp", None),
        P("grp"),
        P("grp"),
        P(("grp", "req"), "tp", None, None),
        P(("grp", "req"), None, "tp"),
        P(("grp", "req"), None, None, "tp"),
        P(("grp", "req"), None, "tp"),
        P(("grp", "req"), None, None, "tp"),
        P(("grp", "req"), None, "tp"),
        P(("grp", "req"), None, "tp"),
        P("tp"),
        P("tp"),
        P("tp"),
        P(None, "tp"),
        P(None, None, "tp"),
        P("tp"),
        P(None, "tp"),
        P("tp"),
    )
    return jax.shard_map(
        body,
        mesh=mesh,
        in_specs=placed,
        out_specs=(P(("grp", "req"), None, "tp"), P(("grp", "req"), None, "tp", None)),
        check_vma=False,
    )
```

profile of v0, /device:TPU:0, one launch (start us, length us, event | category | flops | bytes accessed | tf_op | source)
XLA Modules:
  0.0 174.3 jit_solution(18065320189614660141)
XLA Ops:
  7.2 0.0 copy-start
  7.2 2.8 %convert_element_type.166 = bf16[1,32,64,256]{3,2,1,0:T(8,128)(2,1)} convert(f32[1,32,64,256]{3,2,1,0:T(8,128)} %param.31) | non-fusion elementwise | flops 524288 | bytes 3145728 | tf_op jit(solution)/shard_map/convert_element_type | solution.py:260
  10.0 6.3 %all-to-all-start = ((bf16[4,512,256]{2,1,0:T(8,128)(2,1)}), bf16[4,512,256]{2,1,0:T(8,128)(2,1)}, u32[]{:S(2)}, u32[]{:S(2)}) async-start(bf16[4,512,256]{2,1,0:T(8,128)(2,1)} %bitcast.10), calls=%async_computation | async-start | bytes 2097152 | tf_op jit(solution)/shard_map/all_to_all | solution.py:261
  16.3 1.9 %convolution_bitcast_fusion = f32[4096,128]{0,1:T(8,128)} fusion(bf16[4096,128]{1,0:T(8,128)(2,1)S(1)} %bitcast.83), kind=kOutput, calls=%fused_computation.2 | convolution fusion | flops 134791168 | bytes 3145728 | tf_op jit(solution)/shard_map/dot_general | solution.py:27
  18.2 1.9 %copy.54 = f32[4096,128]{1,0:T(8,128)S(1)} copy(f32[4096,128]{0,1:T(8,128)} %convolution_bitcast_fusion) | data formatting | bytes 4194304 | tf_op jit(solution)/shard_map/reshape | solution.py:30
  20.1 0.0 copy-start.22
  20.2 1.5 multiply_convert_fusion.2
  21.7 0.0 all-gather.4.cloned.1.call-update
  21.8 0.6 dynamic_slice.15
  23.7 46.4 %all-gather.1 = bf16[4,3,3072]{2,1,0:T(4,128)(2,1)S(1)} all-gather(bf16[1,3,3072]{2,1,0:T(4,128)(2,1)S(1)} %maximum_bitcast_fusion), channel_id=2, replica_groups=mesh['grp'=2,'req'=4,'tp'=4] {'req'}, dimensions={0}, use_global_device_ids=true | all-gather | bytes 92160 | tf_op jit(solution)/shard_map/all_gather | solution.py:256
  70.9 0.1 copy_bitcast_fusion.3
  71.0 0.6 reduce-window.6
  71.6 0.2 slice_reduce_fusion
  71.9 0.7 fusion.49
  72.6 0.1 copy_bitcast_fusion
  72.8 0.1 maximum_convert_fusion.1
  72.9 0.1 exponential_bitcast_fusion
  72.9 0.2 copy-done.8
  73.1 0.3 maximum_convert_fusion
  73.4 0.1 copy-done.10
  73.6 2.7 %fusion.11 = f32[256,2048]{1,0:T(8,128)} fusion(f32[259,2048]{1,0:T(8,128)S(1)} %maximum_convert_fusion, f32[2048]{0:T(1024)S(1)} %bitcast.101, f32[2048]{0:T(1024)S(1)} %bitcast.103, f32[2048]{0:T(1024)S(1)} %bitcast.99, f32[2048]{0:T(1024)S(1)} %bitcast.97, f32[2048]{0:T(1024)S(1)} %convert_element_type.168), kind=kLoop, calls=%fused_computation.23 | loop fusion | flops 7340032 | bytes 10526720 | tf_op jit(solution)/shard_map/convert_element_type | solution.py:61
  76.3 0.1 add.128
  76.4 3.0 %copy.43 = f32[256,2048]{0,1:T(8,128)} copy(f32[256,2048]{1,0:T(8,128)} %fusion.11) | data formatting | bytes 4194304 | tf_op jit(solution)/shard_map/convert_element_type | solution.py:61
  79.4 0.6 reduce_window_sum.25
  80.1 0.1 maximum_convert_fusion.2
  80.2 0.7 compare_select_fusion.1
  80.9 0.3 multiply_convert_fusion.7.c_ref
  81.3 0.3 multiply_convert_fusion.6
  81.6 1.1 fusion.20
  82.7 3.0 %gather_fusion = bf16[4,512,256]{2,1,0:T(8,128)(2,1)} fusion(bf16[4,512,256]{2,1,0:T(8,128)(2,1)} %all-to-all-done, s32[1024]{0:T(1024)S(1)} %pad_clamp_fusion), kind=kCustom, calls=%fused_computation | custom fusion | bytes 2097168 | tf_op jit(solution)/shard_map/jit(_take)/gather | solution.py:262
  85.6 4.4 %all-to-all-start.1 = ((bf16[4,512,256]{2,1,0:T(8,128)(2,1)}), bf16[4,512,256]{2,1,0:T(8,128)(2,1)}, u32[]{:S(2)}, u32[]{:S(2)}) async-start(bf16[4,512,256]{2,1,0:T(8,128)(2,1)} %gather_fusion), calls=%async_computation.1 | async-start | bytes 2097152 | tf_op jit(solution)/shard_map/all_to_all | solution.py:265
  90.1 5.1 %fusion = f32[2,16,64,256]{3,2,1,0:T(8,128)} fusion(f32[2,16,256]{2,1,0:T(8,128)} %reduce_window_sum.25, f32[2,256,256]{2,1,0:T(8,128)} %fusion.20, pred[256,256]{1,0:T(8,128)(4,1)S(1)} %iota_compare_fusion, f32[256,2,16,64]{0,3,2,1:T(8,128)S(1)} %bitcast.90, f32[256,2,16]{0,2,1:T(8,128)} %compare_select_fusion.1), kind=kOutput, calls=%fused_computation.3 | convolution fusion | flops 277872640 | bytes 4849664 | tf_op jit(solution)/shard_map/gkts,sgkp->tgkp/dot_general | solution.py:63
  95.1 3.0 %copy.49 = f32[256,2048]{1,0:T(8,128)} copy(f32[256,2048]{0,1:T(8,128)} %bitcast.91) | data formatting | bytes 4194304 | tf_op jit(solution)/shard_map/reshape | solution.py:68
  98.2 0.1 broadcast_in_dim.79
  98.2 0.1 mul.223
  98.3 0.2 broadcast_in_dim.80
  98.5 1.9 %copy.51.decay_ref = f32[256,2048]{1,0:T(8,128)} copy(f32[256,2048]{0,1:T(8,128)S(1)} %bitcast.89) | data formatting | bytes 4194304 | tf_op jit(solution)/shard_map/reshape | solution.py:70
  100.4 0.7 dynamic_slice.17.live_ref
  101.1 1.7 copy.78
  102.8 0.7 compare_select_fusion.2.rows_ref
  103.5 5.7 %multiply_add_fusion.near_ref = f32[256,2048]{1,0:T(8,128)S(1)} fusion(f32[256,2048]{1,0:T(8,128)} %copy.49, f32[2048]{0:T(1024)S(1)} %mul.223, f32[259,2048]{1,0:T(8,128)} %copy-done.5, f32[2048]{0:T(1024)S(1)} %bitcast.102, f32[2048]{0:T(1024)S(1)} %bitcast.104, f32[2048]{0:T(1024)S(1)} %bitcast.100, f32[2048]{0:T(1024)S(1)} %bitcast.98, ...), kind=kLoop, calls=%fused_computation.18 | loop fusion | flops 8388608 | bytes 12632064 | tf_op jit(solution)/shard_map/add | solution.py:69
  109.2 21.9 %all-to-all-done.1 = bf16[4,512,256]{2,1,0:T(8,128)(2,1)} async-done(((bf16[4,512,256]{2,1,0:T(8,128)(2,1)}), bf16[4,512,256]{2,1,0:T(8,128)(2,1)}, u32[]{:S(2)}, u32[]{:S(2)}) %all-to-all-start.1) | async-done | bytes 1048608 | tf_op jit(solution)/shard_map/all_to_all | solution.py:265
  131.2 1.2 copy-done.1
  132.4 3.6 %shard_map.230 = bf16[256,2048]{1,0:T(8,128)(2,1)} custom-call(bf16[256,512]{1,0:T(8,128)(2,1)S(1)} %multiply_convert_fusion.7.c_ref, bf16[2048,256]{1,0:T(8,128)(2,1)} %bitcast.11.state_ref, f32[256,2048]{1,0:T(8,128)S(1)} %multiply_add_fusion.near_ref, f32[256,2048]{1,0:T(8,128)} %copy.51.decay_ref, bf16[256,2048]{1,0:T(8,128)(2,1)S(1)} %bitcast.85, ...), custom_call_target="tpu_custom_call" | custom-call | flops 268435456 | bytes 7340032 | tf_op jit(solution)/shard_map/pallas_call | solution.py:93
  136.0 0.9 copy-done.2
  136.9 2.2 %copy-done.3 = bf16[32,2,2,128,128]{4,3,2,1,0:T(8,128)(2,1)S(1)} copy-done((bf16[32,2,2,128,128]{4,3,2,1,0:T(8,128)(2,1)S(1)}, bf16[32,2,2,128,128]{4,3,2,1,0:T(8,128)(2,1)}, u32[]{:S(2)}) %copy-start.3) | copy-done | bytes 4194328
  139.1 1.2 copy-done.4
  140.3 27.1 %shard_map.231 = bf16[256,16,128]{2,1,0:T(8,128)(2,1)} custom-call(s32[24]{0:T(128)S(1)} %compare_select_fusion.2.rows_ref, s32[1]{0:T(128)} %dynamic_slice.17.live_ref, bf16[256,16,128]{2,1,0:T(8,128)(2,1)S(1)} %bitcast.87, bf16[2,2,256,128]{3,2,1,0:T(8,128)(2,1)S(1)} %bitcast.86, bf16[32,2,2,128,128]{4,3,2,1,0:T(8,128)(2,1)S(1)} %copy-done.3), custom_call_target="tpu_custom_call" | custom-call | flops 13958643712 | bytes 6291456 | tf_op jit(solution)/shard_map/pallas_call | solution.py:191
  (65 shorter events, 0.4 us)
Async XLA Ops:
  7.2 9.1 %copy-start = (bf16[8,2,2,128,128]{4,3,2,1,0:T(8,128)(2,1)S(1)}, bf16[8,2,2,128,128]{4,3,2,1,0:T(8,128)(2,1)}, u32[]{:S(2)}) copy-start(bf16[8,2,2,128,128]{4,3,2,1,0:T(8,128)(2,1)} %param.25) | copy-start | bytes 3145732
  10.0 72.7 %all-to-all-start = ((bf16[4,512,256]{2,1,0:T(8,128)(2,1)}), bf16[4,512,256]{2,1,0:T(8,128)(2,1)}, u32[]{:S(2)}, u32[]{:S(2)}) async-start(bf16[4,512,256]{2,1,0:T(8,128)(2,1)} %bitcast.10), calls=%async_computation | async-start | bytes 2097152 | tf_op jit(solution)/shard_map/all_to_all | solution.py:261
  16.3 119.7 %all-gather.4.cloned.1.call-start = ((), (), s32[]{:S(2)}) async-start(), calls=%async_computation.2 | async-start | bytes 5242880 | tf_op jit(solution)/shard_map/all_gather | solution.py:248
  18.2 1.9 %copy-start.14 = (bf16[8,2,2,128]{3,2,1,0:T(2,128)(2,1)S(1)}, bf16[8,2,2,128]{3,2,1,0:T(2,128)(2,1)}, u32[]{:S(2)}) copy-start(bf16[8,2,2,128]{3,2,1,0:T(2,128)(2,1)} %param.26) | copy-start | bytes 24580
  20.1 1.6 copy-start.22
  20.2 3.5 %copy-start.12 = (bf16[1,3,2,512]{3,2,1,0:T(2,128)(2,1)S(1)}, bf16[1,3,2,512]{3,2,1,0:T(2,128)(2,1)}, u32[]{:S(2)}) copy-start(bf16[1,3,2,512]{3,2,1,0:T(2,128)(2,1)} %param.33) | copy-start | bytes 18436
  20.2 3.5 %copy-start.13 = (bf16[1,3,2048]{2,1,0:T(4,128)(2,1)S(1)}, bf16[1,3,2048]{2,1,0:T(4,128)(2,1)}, u32[]{:S(2)}) copy-start(bf16[1,3,2048]{2,1,0:T(4,128)(2,1)} %param.32) | copy-start | bytes 36868
  20.2 50.7 %copy-start.16 = (bf16[2048]{0:T(1024)(128)(2,1)S(1)}, bf16[2048]{0:T(1024)(128)(2,1)}, u32[]{:S(2)}) copy-start(bf16[2048]{0:T(1024)(128)(2,1)} %param.43) | copy-start | bytes 12292
  20.2 50.7 %copy-start.9 = (f32[1,256,32]{1,2,0:T(8,128)S(1)}, f32[1,256,32]{1,2,0:T(8,128)}, u32[]{:S(2)}) copy-start(f32[1,256,32]{1,2,0:T(8,128)} %param.37) | copy-start | bytes 98308
  20.2 50.7 %copy-start.20 = (f32[32]{0:T(128)S(1)}, f32[32]{0:T(128)}, u32[]{:S(2)}) copy-start(f32[32]{0:T(128)} %param.39) | copy-start | bytes 388
  20.2 50.7 %copy-start.21 = (f32[32]{0:T(128)S(1)}, f32[32]{0:T(128)}, u32[]{:S(2)}) copy-start(f32[32]{0:T(128)} %param.38) | copy-start | bytes 388
  21.7 50.2 %copy-start.7 = (bf16[1,256,2,512]{3,2,1,0:T(2,128)(2,1)S(1)}, bf16[1,256,2,512]{3,2,1,0:T(2,128)(2,1)}, u32[]{:S(2)}) copy-start(bf16[1,256,2,512]{3,2,1,0:T(2,128)(2,1)} %param.35) | copy-start | bytes 1572868
  71.9 1.2 copy-start.8
  72.8 0.8 copy-start.10
  73.6 2.7 %copy-start.5 = (f32[259,2048]{1,0:T(8,128)}, f32[259,2048]{1,0:T(8,128)S(1)}, u32[]{:S(2)}) copy-start(f32[259,2048]{1,0:T(8,128)S(1)} %maximum_convert_fusion) | copy-start | bytes 6365188
  76.4 3.8 %copy-start.15 = (bf16[2,512]{1,0:T(2,128)(2,1)S(1)}, bf16[2,512]{1,0:T(2,128)(2,1)}, u32[]{:S(2)}) copy-start(bf16[2,512]{1,0:T(2,128)(2,1)} %param.44) | copy-start | bytes 6148
  76.4 3.8 %copy-start.11 = (bf16[4,2,512]{2,1,0:T(2,128)(2,1)S(1)}, bf16[4,2,512]{2,1,0:T(2,128)(2,1)}, u32[]{:S(2)}) copy-start(bf16[4,2,512]{2,1,0:T(2,128)(2,1)} %param.42) | copy-start | bytes 24580
  82.7 7.4 %copy-start.6 = (f32[256,2048]{0,1:T(8,128)S(1)}, f32[256,2048]{0,1:T(8,128)}, u32[]{:S(2)}) copy-start(f32[256,2048]{0,1:T(8,128)} %copy.43) | copy-start | bytes 6291460
  85.6 45.5 %all-to-all-start.1 = ((bf16[4,512,256]{2,1,0:T(8,128)(2,1)}), bf16[4,512,256]{2,1,0:T(8,128)(2,1)}, u32[]{:S(2)}, u32[]{:S(2)}) async-start(bf16[4,512,256]{2,1,0:T(8,128)(2,1)} %gather_fusion), calls=%async_computation.1 | async-start | bytes 2097152 | tf_op jit(solution)/shard_map/all_to_all | solution.py:265
  95.1 3.0 %copy-start.23 = (f32[32]{0:T(128)S(1)}, f32[32]{0:T(128)}, u32[]{:S(2)}) copy-start(f32[32]{0:T(128)} %param.40) | copy-start | bytes 388
  98.5 1.9 %copy-start.17 = (bf16[2048]{0:T(1024)(128)(2,1)S(1)}, bf16[2048]{0:T(1024)(128)(2,1)}, u32[]{:S(2)}) copy-start(bf16[2048]{0:T(1024)(128)(2,1)} %param.45) | copy-start | bytes 12292
  98.5 1.9 %copy-start.24 = (s32[4]{0:T(128)S(1)}, s32[4]{0:T(128)}, u32[]{:S(2)}) copy-start(s32[4]{0:T(128)} %param.29) | copy-start | bytes 52
  98.5 4.3 %copy-start.18 = (s32[4,24]{1,0:T(4,128)S(1)}, s32[4,24]{1,0:T(4,128)}, u32[]{:S(2)}) copy-start(s32[4,24]{1,0:T(4,128)} %param.28) | copy-start | bytes 1156
  98.5 4.3 %copy-start.19 = (s32[4,24]{1,0:T(4,128)S(1)}, s32[4,24]{1,0:T(4,128)}, u32[]{:S(2)}) copy-start(s32[4,24]{1,0:T(4,128)} %param.27) | copy-start | bytes 1156
  131.2 1.2 copy-start.1
  136.0 1.0 copy-start.2
  136.9 2.2 %copy-start.3 = (bf16[32,2,2,128,128]{4,3,2,1,0:T(8,128)(2,1)S(1)}, bf16[32,2,2,128,128]{4,3,2,1,0:T(8,128)(2,1)}, u32[]{:S(2)}) copy-start(bf16[32,2,2,128,128]{4,3,2,1,0:T(8,128)(2,1)} %all-gather.4.cloned.1.call-done.pool_ref) | copy-start | bytes 12582916
  139.1 1.2 copy-start.4
Sparse Core Ops, SparseCore 0:
  21.9 112.1 all-gather.3
where the time goes:
time: 175 us; the launch traced here: 174 us
  blocking collectives  46.4 us (27%)
  Pallas kernels  30.7 us (18%)
  local copies, waits for them, and re-layouts  23.9 us (14%)
  waiting for transfers between devices  22 us (13%)
  between operations  16.4 us (9%)
  other arithmetic  16.1 us (9%)
  starting transfers between devices  10.7 us (6%)
  matrix products  8.02 us (5%)
    all_gather x1, blocking collectives, body(): all_history = lax.all_gather(history, 'req', axis=0)  46.4 us
    pallas_call x1, Pallas kernels, attend(): pl.pallas_call(attend_kernel, grid_spec=pltpu.PrefetchScalarGridSpec(num_...  27.1 us
    all_to_all x1, waiting for transfers between devices, body(): lax.all_to_all(chosen, 'req', split_axis=0, concat_axis=0, tiled=True)  21.9 us
    unnamed x52, local copies, waits for them, and re-layouts  7.72 us
    all_to_all x1, starting transfers between devices, body(): lax.all_to_all(state_rows, 'req', split_axis=0, concat_axis=0, tiled=True)  6.32 us
    add x1, other arithmetic, ssm_before_state(): intra_term + jnp.repeat(skip_gain, head_dim)[None, :] * conv_x.astype(F32)  5.67 us
    dot_general x1, matrix products, ssm_before_state(): jnp.einsum('gkts,sgkp->tgkp', mix_rows, scaled_x.reshape(length, groups,...  5.08 us
    all_to_all x1, starting transfers between devices, body(): lax.all_to_all(chosen, 'req', split_axis=0, concat_axis=0, tiled=True)  4.42 us
  transfers between devices with their start and end apart: 3, of which 1 were waited for; matrix products, arithmetic and copies ran while one was open for 23% of the time, Pallas kernels for 2%

commit v1 on v0

--- a/solution.py
+++ b/solution.py
@@ -71,7 +71,7 @@
     return near, decay
 
 
-def tail_kernel(c_ref, state_ref, near_ref, decay_ref, z_ref, gain_ref, out_ref):
+def tail_kernel(c_ref, state_ref, near_ref, decay_ref, z_ref, gain_ref, after_ref, out_ref):
     carried = lax.dot_general(
         c_ref[...], state_ref[...], (((1,), (1,)), ((), ())), preferred_element_type=F32
     )
@@ -84,7 +84,7 @@
     ).astype(BF16)
 
 
-def ssm_tail(c_rows, state, near, decay, gate_rows, norm_gain):
+def ssm_tail(c_rows, state, near, decay, gate_rows, norm_gain, after):
     length, width = gate_rows.shape
     state_dim = state.shape[1]
     groups = c_rows.shape[1] // state_dim
@@ -101,6 +101,7 @@
             wide,
             wide,
             pl.BlockSpec((1, span), lambda g: (0, g)),
+            pl.BlockSpec(memory_space=pl.ANY),
         ],
         out_specs=wide,
         compiler_params=pltpu.CompilerParams(vmem_limit_bytes=VMEM_LIMIT),
@@ -109,10 +110,36 @@
             bytes_accessed=length * width * 12 + width * state_dim * 2,
             transcendentals=length * width,
         ),
-    )(c_rows, state, near, decay, gate_rows, norm_gain.reshape(1, -1))
-
-
-def attend_kernel(rows_ref, live_ref, q_ref, new_ref, pool_ref, out_ref, key_buf, val_buf):
+    )(c_rows, state, near, decay, gate_rows, norm_gain.reshape(1, -1), after)
+
+
+def choose_kernel(owner_ref, piece_ref, pool_ref, near_ref, out_ref):
+    out_ref[...] = piece_ref[...]
+
+
+def choose_pieces(state_owner, spread, piece_rows, pool, near):
+    owners, _, state_dim = spread.shape
+    block = (1, piece_rows, state_dim)
+    return pl.pallas_call(
+        choose_kernel,
+        grid_spec=pltpu.PrefetchScalarGridSpec(
+            num_scalar_prefetch=1,
+            grid=(owners,),
+            in_specs=[
+                pl.BlockSpec(block, lambda i, owner: (owner[i], 0, 0)),
+                pl.BlockSpec(memory_space=pl.ANY),
+                pl.BlockSpec(memory_space=pl.ANY),
+            ],
+            out_specs=pl.BlockSpec(block, lambda i, owner: (i, 0, 0)),
+        ),
+        out_shape=jax.ShapeDtypeStruct((owners, piece_rows, state_dim), BF16),
+        compiler_params=pltpu.CompilerParams(vmem_limit_bytes=VMEM_LIMIT),
+    )(state_owner, spread, pool, near)
+
+
+def attend_kernel(
+    rows_ref, live_ref, q_ref, new_ref, pool_ref, after_ref, out_ref, key_buf, val_buf
+):
     kv_here = new_ref.shape[1]
     length = new_ref.shape[2]
     width = new_ref.shape[3]
@@ -181,7 +208,7 @@
     out_ref[...] = jnp.concatenate(parts, axis=1).astype(BF16)
 
 
-def attend(query_rows, new_rows, pool, rows, live):
+def attend(query_rows, new_rows, pool, rows, live, after):
     length, heads_here, width = query_rows.shape
     kv_here = new_rows.shape[1]
     table_len = rows.shape[0]
@@ -197,6 +224,7 @@
                 pl.BlockSpec((tile, heads_here, width), lambda i, *_: (i, 0, 0)),
                 pl.BlockSpec(new_rows.shape, whole),
                 pl.BlockSpec(memory_space=pltpu.VMEM),
+                pl.BlockSpec(memory_space=pl.ANY),
             ],
             out_specs=pl.BlockSpec((tile, heads_here, width), lambda i, *_: (i, 0, 0)),
             scratch_shapes=[
@@ -211,7 +239,7 @@
             bytes_accessed=pool.size * 2 + 4 * query_rows.size,
             transcendentals=length * heads_here * keys,
         ),
-    )(rows, live, query_rows, new_rows, pool)
+    )(rows, live, query_rows, new_rows, pool, after)
 
 
 def body(
@@ -253,16 +281,25 @@
     history = jnp.concatenate(
         [conv_pool_x[0], conv_pool_bc[0, :, 0], conv_pool_bc[0, :, 1]], axis=1
     )
-    all_history = lax.all_gather(history, "req", axis=0)
+    flat_rows = -(-history.size // state_dim)
+    pad_rows = -(-flat_rows // 16) * 16
+    flat_history = jnp.pad(history.reshape(-1), (0, pad_rows * state_dim - history.size))
+    state_pieces = ssm_pool[0].astype(BF16).reshape(owners, -1, state_dim)
+    piece_rows = state_pieces.shape[1]
+    outgoing = jnp.concatenate(
+        [
+            state_pieces,
+            jnp.broadcast_to(
+                flat_history.reshape(1, pad_rows, state_dim), (owners, pad_rows, state_dim)
+            ),
+        ],
+        axis=1,
+    )
+    spread = lax.all_to_all(outgoing, "req", split_axis=0, concat_axis=0, tiled=True)
     my_source = lax.dynamic_index_in_dim(state_owner, my_index, 0, keepdims=False)
-    my_history = lax.dynamic_index_in_dim(all_history, my_source, 0, keepdims=False)
-
-    state_rows = ssm_pool[0].reshape(-1, state_dim).astype(BF16)
-    spread = lax.all_to_all(state_rows, "req", split_axis=0, concat_axis=0, tiled=True)
-    chosen = jnp.take(
-        spread.reshape(owners, -1, state_dim), state_owner, axis=0, mode="clip"
-    ).reshape(-1, state_dim)
-    state = lax.all_to_all(chosen, "req", split_axis=0, concat_axis=0, tiled=True)
+    my_history = lax.dynamic_slice(
+        spread, (my_source, piece_rows, 0), (1, pad_rows, state_dim)
+    ).reshape(-1)[: history.size].reshape(history.shape)
 
     conv_x = causal_conv(my_history[:, :rows_x], x_in[0], conv_weight_x, conv_bias_x)
     conv_b = causal_conv(
@@ -278,14 +315,18 @@
         conv_x, conv_b, conv_c, dt_raw[0], dt_bias, ssm_rate, skip_gain, state_dim
     )
 
+    chosen = choose_pieces(state_owner, spread, piece_rows, pool, near)
+    state = lax.all_to_all(chosen, "req", split_axis=0, concat_axis=0, tiled=True)
+    state = state.reshape(-1, state_dim)
+
     live = lax.dynamic_slice_in_dim(prefix_blocks, my_index, 1, 0)
     table = block_owner * held + block_index
     my_table = lax.dynamic_index_in_dim(table, my_index, 0, keepdims=False)
     rows = jnp.where(jnp.arange(my_table.shape[0]) < live, my_table, my_table[0])
     new_rows = kv_new[0].transpose(1, 2, 0, 3)
-    attended = attend(queries[0], new_rows, pool, rows, live)
-
-    ssm_rows = ssm_tail(conv_c, state, near, decay, z_in[0], norm_gain)
+    attended = attend(queries[0], new_rows, pool, rows, live, chosen)
+
+    ssm_rows = ssm_tail(conv_c, state, near, decay, z_in[0], norm_gain, attended)
     return (ssm_rows[None], attended[None])
 
 

time: 175 us -> 181 us (1.034)
  blocking collectives: 46.4 us -> 0 us
  waiting for transfers between devices: 22 us -> 62.4 us
  local copies, waits for them, and re-layouts: 23.9 us -> 32.6 us
  matrix products: 8.02 us -> 4.21 us
  other arithmetic: 16.1 us -> 19.4 us
  Pallas kernels: 30.7 us -> 33.7 us
    all_to_all x1, waiting for transfers between devices: 0.01 us -> 49.3 us  [body(): lax.all_to_all(outgoing, 'req', split_axis=0, concat_axis=0, tiled=True)]
    all_gather x1 -> x0, blocking collectives: 46.4 us -> none  [body(): all_history = lax.all_gather(history, 'req', axis=0)]
    all_to_all x1, waiting for transfers between devices: 21.9 us -> 0.01 us  [body(): lax.all_to_all(chosen, 'req', split_axis=0, concat_axis=0, tiled=True)]
    all_gather x1, waiting for transfers between devices: 0.01 us -> 13.1 us  [body(): pool = lax.all_gather(own_blocks, 'req', axis=0, tiled=True)]
    unnamed x52 -> x102, local copies, waits for them, and re-layouts: 7.72 us -> 13.4 us
    dot_general x1, matrix products: 5.08 us -> 2.1 us  [ssm_before_state(): jnp.einsum('gkts,sgkp->tgkp', mix_rows, scaled_x.reshape(length, groups,...]
    gather x1 -> x0, local copies, waits for them, and re-layouts: 2.96 us -> none  [body(): jnp.take(spread.reshape(owners, -1, state_dim), state_owner, axis=0, mode...]
    pallas_call x1, Pallas kernels: 27.1 us -> 29.5 us  [attend(): pl.pallas_call(attend_kernel, grid_spec=pltpu.PrefetchScalarGridSpec(num_...]
  transfers between devices with their start and end apart: 3 -> 3, of which waited for: 1 -> 2; matrix products, arithmetic and copies ran while one was open for 23% -> 22% of each run, Pallas kernels for 2% -> 16%
where the time goes in v1:
time: 181 us; the launch traced here: 180 us
  waiting for transfers between devices  62.4 us (34%)
  Pallas kernels  33.7 us (19%)
  local copies, waits for them, and re-layouts  32.6 us (18%)
  other arithmetic  19.4 us (11%)
  between operations  16.6 us (9%)
  starting transfers between devices  10.9 us (6%)
  matrix products  4.21 us (2%)
    all_to_all x1, waiting for transfers between devices, body(): lax.all_to_all(outgoing, 'req', split_axis=0, concat_axis=0, tiled=True)  49.3 us
    pallas_call x1, Pallas kernels, attend(): pl.pallas_call(attend_kernel, grid_spec=pltpu.PrefetchScalarGridSpec(num_...  29.5 us
    unnamed x102, local copies, waits for them, and re-layouts  13.4 us
    all_gather x1, waiting for transfers between devices, body(): pool = lax.all_gather(own_blocks, 'req', axis=0, tiled=True)  13.1 us
    all_to_all x1, starting transfers between devices, body(): lax.all_to_all(outgoing, 'req', split_axis=0, concat_axis=0, tiled=True)  6.32 us
    add x1, other arithmetic, ssm_before_state(): intra_term + jnp.repeat(skip_gain, head_dim)[None, :] * conv_x.astype(F32)  5.69 us
    all_to_all x1, starting transfers between devices, body(): lax.all_to_all(chosen, 'req', split_axis=0, concat_axis=0, tiled=True)  4.56 us
  transfers between devices with their start and end apart: 3, of which 2 were waited for; matrix products, arithmetic and copies ran while one was open for 22% of the time, Pallas kernels for 16%

profile of v1, /device:TPU:0, one launch (start us, length us, event | category | flops | bytes accessed | tf_op | source)
XLA Modules:
  0.0 179.9 jit_solution(16829021437130856343)
XLA Ops:
  7.2 1.2 copy-done
  8.4 1.9 %convolution_bitcast_fusion = f32[4096,128]{0,1:T(8,128)} fusion(bf16[4096,128]{1,0:T(8,128)(2,1)S(1)} %bitcast.79), kind=kOutput, calls=%fused_computation.1 | convolution fusion | flops 134791168 | bytes 3145728 | tf_op jit(solution)/shard_map/dot_general | solution.py:27
  10.3 1.9 %copy.54 = f32[4096,128]{1,0:T(8,128)S(1)} copy(f32[4096,128]{0,1:T(8,128)} %convolution_bitcast_fusion) | data formatting | bytes 4194304 | tf_op jit(solution)/shard_map/reshape | solution.py:30
  12.2 1.5 multiply_convert_fusion.4
  13.9 1.7 convert_element_type.160
  15.8 1.1 pad_maximum_fusion
  16.9 6.3 %all-to-all-start = ((bf16[4,560,256]{2,1,0:T(8,128)(2,1)}), bf16[4,560,256]{2,1,0:T(8,128)(2,1)S(1)}, u32[]{:S(2)}, u32[]{:S(2)}) async-start(bf16[4,560,256]{2,1,0:T(8,128)(2,1)} %pad_maximum_fusion), calls=%async_computation | async-start | bytes 2293760 | tf_op jit(solution)/shard_map/all_to_all | solution.py:298
  23.2 0.6 dynamic_slice.14
  25.3 0.6 reduce-window.6
  26.3 0.6 reduce_window_sum.25
  27.0 0.7 mul.227
  28.3 0.6 iota_compare_fusion
  28.9 0.6 slice_convert_fusion.8
  29.5 0.6 slice_convert_fusion.7
  30.2 0.7 compare_select_fusion.1
  30.9 0.7 fusion.49
  31.6 0.8 copy_bitcast_fusion
  32.4 1.5 slice_convert_fusion.3
  33.9 49.3 %all-to-all-done.piece_ref = bf16[4,560,256]{2,1,0:T(8,128)(2,1)S(1)} async-done(((bf16[4,560,256]{2,1,0:T(8,128)(2,1)}), bf16[4,560,256]{2,1,0:T(8,128)(2,1)S(1)}, u32[]{:S(2)}, u32[]{:S(2)}) %all-to-all-start) | async-done | bytes 1146912 | tf_op jit(solution)/shard_map/all_to_all | solution.py:298
  83.2 0.6 constant_dynamic-slice_fusion
  83.9 1.3 reshape.206
  85.2 0.8 slice.173
  86.3 1.4 copy-done.10
  87.7 2.6 %fusion.11 = f32[256,2048]{1,0:T(8,128)} fusion(f32[259,2048]{1,0:T(8,128)S(1)} %maximum_convert_fusion, f32[2048]{0:T(1024)S(1)} %bitcast.99, f32[2048]{0:T(1024)S(1)} %bitcast.101, f32[2048]{0:T(1024)S(1)} %bitcast.97, f32[2048]{0:T(1024)S(1)} %bitcast.95, f32[2048]{0:T(1024)S(1)} %convert_element_type.173), kind=kLoop, calls=%fused_computation.23 | loop fusion | flops 7340032 | bytes 10526720 | tf_op jit(solution)/shard_map/convert_element_type | solution.py:61
  90.4 3.0 %copy.44 = f32[256,2048]{0,1:T(8,128)} copy(f32[256,2048]{1,0:T(8,128)} %fusion.11) | data formatting | bytes 4194304 | tf_op jit(solution)/shard_map/convert_element_type | solution.py:61
  93.4 0.7 fusion.50
  94.3 0.3 multiply_convert_fusion.7.c_ref
  95.3 0.9 copy-done.11
  96.2 2.1 %fusion = f32[2,16,64,256]{3,2,1,0:T(8,128)S(1)} fusion(f32[2,16,256]{2,1,0:T(8,128)S(1)} %copy-done.26, f32[2,256,256]{2,1,0:T(8,128)S(1)} %fusion.20, pred[256,256]{1,0:T(8,128)(4,1)S(1)} %copy-done.24, f32[256,2,16,64]{0,3,2,1:T(8,128)S(1)} %bitcast.88, f32[256,2,16]{0,2,1:T(8,128)S(1)} %copy-done.27), kind=kOutput, calls=%fused_computation.2 | convolution fusion | flops 277872640 | bytes 4849664 | tf_op jit(solution)/shard_map/gkts,sgkp->tgkp/dot_general | solution.py:63
  98.4 1.9 %copy.50 = f32[256,2048]{1,0:T(8,128)} copy(f32[256,2048]{0,1:T(8,128)S(1)} %bitcast.89) | data formatting | bytes 4194304 | tf_op jit(solution)/shard_map/reshape | solution.py:68
  100.3 5.7 %multiply_add_fusion.near_ref = f32[256,2048]{1,0:T(8,128)S(1)} fusion(f32[256,2048]{1,0:T(8,128)} %copy.50, f32[2048]{0:T(1024)S(1)} %copy-done.25, f32[259,2048]{1,0:T(8,128)} %copy-done.10, f32[2048]{0:T(1024)S(1)} %bitcast.100, f32[2048]{0:T(1024)S(1)} %bitcast.102, f32[2048]{0:T(1024)S(1)} %bitcast.98, f32[2048]{0:T(1024)S(1)} %bitcast.96, ...), kind=kLoop, calls=%fused_computation.16 | loop fusion | flops 8388608 | bytes 12632064 | tf_op jit(solution)/shard_map/add | solution.py:69
  106.0 13.1 %all-gather.2.cloned.1.call-done.pool_ref = bf16[32,2,2,128,128]{4,3,2,1,0:T(8,128)(2,1)} async-done(((bf16[8,2,2,128,128]{4,3,2,1,0:T(8,128)(2,1)}), bf16[32,2,2,128,128]{4,3,2,1,0:T(8,128)(2,1)}) %all-gather.2.cloned.1.call-update) | async-done | bytes 4194320 | tf_op jit(solution)/shard_map/all_gather | solution.py:276
  119.1 1.3 copy-done.2
  120.4 0.7 shard_map.230.after_ref
  121.1 1.0 copy-done.3
  122.0 4.6 %all-to-all-start.1 = ((bf16[4,512,256]{2,1,0:T(8,128)(2,1)}), bf16[4,512,256]{2,1,0:T(8,128)(2,1)}, u32[]{:S(2)}, u32[]{:S(2)}) async-start(bf16[4,512,256]{2,1,0:T(8,128)(2,1)} %copy-done.3), calls=%async_computation.1 | async-start | bytes 2097152 | tf_op jit(solution)/shard_map/all_to_all | solution.py:319
  126.6 0.6 dynamic_slice.16.live_ref
  127.3 1.7 copy.78
  129.0 1.5 broadcast_in_dim.86
  130.5 2.9 %copy.53.decay_ref = f32[256,2048]{1,0:T(8,128)} copy(f32[256,2048]{0,1:T(8,128)} %bitcast.86) | data formatting | bytes 4194304 | tf_op jit(solution)/shard_map/reshape | solution.py:70
  133.5 0.7 compare_select_fusion.2.rows_ref
  134.1 1.2 copy-done.4
  135.4 0.9 copy-done.7
  136.3 1.2 copy-done.9
  137.5 29.5 %shard_map.231.after_ref = bf16[256,16,128]{2,1,0:T(8,128)(2,1)} custom-call(s32[24]{0:T(128)S(1)} %compare_select_fusion.2.rows_ref, s32[1]{0:T(128)} %dynamic_slice.16.live_ref, bf16[256,16,128]{2,1,0:T(8,128)(2,1)S(1)} %bitcast.84, bf16[2,2,256,128]{3,2,1,0:T(8,128)(2,1)S(1)} %bitcast.83, ...), custom_call_target="tpu_custom_call" | custom-call | flops 13958643712 | bytes 6291456 | tf_op jit(solution)/shard_map/pallas_call | solution.py:218
  167.0 1.2 copy-done.5
  168.2 1.2 copy-done.6
  169.5 3.6 %shard_map.232 = bf16[256,2048]{1,0:T(8,128)(2,1)} custom-call(bf16[256,512]{1,0:T(8,128)(2,1)S(1)} %multiply_convert_fusion.7.c_ref, bf16[2048,256]{1,0:T(8,128)(2,1)} %bitcast.29.state_ref, f32[256,2048]{1,0:T(8,128)S(1)} %multiply_add_fusion.near_ref, f32[256,2048]{1,0:T(8,128)} %copy.53.decay_ref, bf16[256,2048]{1,0:T(8,128)(2,1)S(1)} %bitcast.81, ...), custom_call_target="tpu_custom_call" | custom-call | flops 268435456 | bytes 7340032 | tf_op jit(solution)/shard_map/pallas_call | solution.py:93
  (119 shorter events, 2.0 us)
Async XLA Ops:
  7.2 1.2 copy-start
  7.2 111.9 %all-gather.2.cloned.1.call-start = ((), (), s32[]{:S(2)}) async-start(), calls=%async_computation.2 | async-start | bytes 5242880 | tf_op jit(solution)/shard_map/all_gather | solution.py:276
  10.3 1.9 %copy-start.31 = (bf16[8,2,2,128]{3,2,1,0:T(2,128)(2,1)S(1)}, bf16[8,2,2,128]{3,2,1,0:T(2,128)(2,1)}, u32[]{:S(2)}) copy-start(bf16[8,2,2,128]{3,2,1,0:T(2,128)(2,1)} %param.26) | copy-start | bytes 24580
  12.2 1.6 copy-start.29
  12.2 1.6 copy-start.30
  15.7 7.6 %copy-start.8 = (s32[4]{0:T(128)S(1)}, s32[4]{0:T(128)}, u32[]{:S(2)}) copy-start(s32[4]{0:T(128)} %owner_ref.1) | copy-start | bytes 52
  15.7 9.4 %copy-start.42 = (bf16[2048]{0:T(1024)(128)(2,1)S(1)}, bf16[2048]{0:T(1024)(128)(2,1)}, u32[]{:S(2)}) copy-start(bf16[2048]{0:T(1024)(128)(2,1)} %param.43) | copy-start | bytes 12292
  15.7 9.4 %copy-start.47 = (f32[32]{0:T(128)S(1)}, f32[32]{0:T(128)}, u32[]{:S(2)}) copy-start(f32[32]{0:T(128)} %param.38) | copy-start | bytes 388
  15.7 9.5 %copy-start.15 = (f32[1,256,32]{1,2,0:T(8,128)S(1)}, f32[1,256,32]{1,2,0:T(8,128)}, u32[]{:S(2)}) copy-start(f32[1,256,32]{1,2,0:T(8,128)} %param.37) | copy-start | bytes 98308
  15.7 9.5 %copy-start.46 = (f32[32]{0:T(128)S(1)}, f32[32]{0:T(128)}, u32[]{:S(2)}) copy-start(f32[32]{0:T(128)} %param.39) | copy-start | bytes 388
  15.7 11.2 %copy-start.48 = (f32[32]{0:T(128)S(1)}, f32[32]{0:T(128)}, u32[]{:S(2)}) copy-start(f32[32]{0:T(128)} %param.40) | copy-start | bytes 388
  15.7 13.2 %copy-start.32 = (bf16[2,512]{1,0:T(2,128)(2,1)S(1)}, bf16[2,512]{1,0:T(2,128)(2,1)}, u32[]{:S(2)}) copy-start(bf16[2,512]{1,0:T(2,128)(2,1)} %param.44) | copy-start | bytes 6148
  15.8 13.8 %copy-start.28 = (bf16[4,2,512]{2,1,0:T(2,128)(2,1)S(1)}, bf16[4,2,512]{2,1,0:T(2,128)(2,1)}, u32[]{:S(2)}) copy-start(bf16[4,2,512]{2,1,0:T(2,128)(2,1)} %param.42) | copy-start | bytes 24580
  15.8 15.1 %copy-start.12 = (bf16[1,256,2,512]{3,2,1,0:T(2,128)(2,1)S(1)}, bf16[1,256,2,512]{3,2,1,0:T(2,128)(2,1)}, u32[]{:S(2)}) copy-start(bf16[1,256,2,512]{3,2,1,0:T(2,128)(2,1)} %param.35) | copy-start | bytes 1572868
  16.9 66.3 %all-to-all-start = ((bf16[4,560,256]{2,1,0:T(8,128)(2,1)}), bf16[4,560,256]{2,1,0:T(8,128)(2,1)S(1)}, u32[]{:S(2)}, u32[]{:S(2)}) async-start(bf16[4,560,256]{2,1,0:T(8,128)(2,1)} %pad_maximum_fusion), calls=%async_computation | async-start | bytes 2293760 | tf_op jit(solution)/shard_map/all_to_all | solution.py:298
  31.6 54.4 %copy-start.13 = (bf16[1,256,2048]{2,1,0:T(8,128)(2,1)S(1)}, bf16[1,256,2048]{2,1,0:T(8,128)(2,1)}, u32[]{:S(2)}) copy-start(bf16[1,256,2048]{2,1,0:T(8,128)(2,1)} %param.34) | copy-start | bytes 3145732
  83.2 7.1 %copy-start.1 = (bf16[4,560,256]{2,1,0:T(8,128)(2,1)}, bf16[4,560,256]{2,1,0:T(8,128)(2,1)S(1)}, u32[]{:S(2)}) copy-start(bf16[4,560,256]{2,1,0:T(8,128)(2,1)S(1)} %all-to-all-done.piece_ref) | copy-start | bytes 3440644
  85.2 2.5 %copy-start.16 = (f32[1,2048]{1,0:T(1,128)S(1)}, f32[1,2048]{1,0:T(1,128)}, u32[]{:S(2)}) copy-start(f32[1,2048]{1,0:T(1,128)} %get-tuple-element.8) | copy-start | bytes 24580
  85.2 2.5 %copy-start.18 = (f32[1,2048]{1,0:T(1,128)S(1)}, f32[1,2048]{1,0:T(1,128)}, u32[]{:S(2)}) copy-start(f32[1,2048]{1,0:T(1,128)} %get-tuple-element.9) | copy-start | bytes 24580
  85.2 2.5 %copy-start.20 = (f32[1,2048]{1,0:T(1,128)S(1)}, f32[1,2048]{1,0:T(1,128)}, u32[]{:S(2)}) copy-start(f32[1,2048]{1,0:T(1,128)} %get-tuple-element.10) | copy-start | bytes 24580
  85.2 2.5 %copy-start.22 = (f32[1,2048]{1,0:T(1,128)S(1)}, f32[1,2048]{1,0:T(1,128)}, u32[]{:S(2)}) copy-start(f32[1,2048]{1,0:T(1,128)} %get-tuple-element.11) | copy-start | bytes 24580
  86.3 1.4 copy-start.10
  90.3 3.8 %copy-start.14 = (bf16[256,512]{1,0:T(8,128)(2,1)S(1)}, bf16[256,512]{1,0:T(8,128)(2,1)}, u32[]{:S(2)}) copy-start(bf16[256,512]{1,0:T(8,128)(2,1)} %get-tuple-element.25) | copy-start | bytes 786436
  90.3 3.9 %copy-start.36 = (f32[1,1,512]{2,1,0:T(1,128)S(1)}, f32[1,1,512]{2,1,0:T(1,128)}, u32[]{:S(2)}) copy-start(f32[1,1,512]{2,1,0:T(1,128)} %get-tuple-element.14) | copy-start | bytes 6148
  90.3 3.9 %copy-start.37 = (f32[1,1,512]{2,1,0:T(1,128)S(1)}, f32[1,1,512]{2,1,0:T(1,128)}, u32[]{:S(2)}) copy-start(f32[1,1,512]{2,1,0:T(1,128)} %get-tuple-element.15) | copy-start | bytes 6148
  90.3 3.9 %copy-start.38 = (f32[1,1,512]{2,1,0:T(1,128)S(1)}, f32[1,1,512]{2,1,0:T(1,128)}, u32[]{:S(2)}) copy-start(f32[1,1,512]{2,1,0:T(1,128)} %get-tuple-element.16) | copy-start | bytes 6148
  90.3 3.9 %copy-start.39 = (f32[1,1,512]{2,1,0:T(1,128)S(1)}, f32[1,1,512]{2,1,0:T(1,128)}, u32[]{:S(2)}) copy-start(f32[1,1,512]{2,1,0:T(1,128)} %get-tuple-element.17) | copy-start | bytes 6148
  90.3 3.9 %copy-start.41 = (f32[1,512]{1,0:T(1,128)S(1)}, f32[1,512]{1,0:T(1,128)}, u32[]{:S(2)}) copy-start(f32[1,512]{1,0:T(1,128)} %get-tuple-element.23) | copy-start | bytes 6148
  93.4 1.3 copy-start.33
  93.4 1.3 copy-start.34
  93.4 1.3 copy-start.35
  93.4 1.3 copy-start.40
  94.6 1.6 copy-start.11
  94.7 1.6 copy-start.24
  94.7 1.6 copy-start.26
  94.7 1.6 copy-start.27
  98.3 2.0 %copy-start.17 = (f32[1,2048]{1,0:T(1,128)S(1)}, f32[1,2048]{1,0:T(1,128)}, u32[]{:S(2)}) copy-start(f32[1,2048]{1,0:T(1,128)} %get-tuple-element.8) | copy-start | bytes 24580
  98.4 2.0 %copy-start.19 = (f32[1,2048]{1,0:T(1,128)S(1)}, f32[1,2048]{1,0:T(1,128)}, u32[]{:S(2)}) copy-start(f32[1,2048]{1,0:T(1,128)} %get-tuple-element.9) | copy-start | bytes 24580
  98.4 1.9 %copy-start.21 = (f32[1,2048]{1,0:T(1,128)S(1)}, f32[1,2048]{1,0:T(1,128)}, u32[]{:S(2)}) copy-start(f32[1,2048]{1,0:T(1,128)} %get-tuple-element.10) | copy-start | bytes 24580
  98.4 1.9 %copy-start.23 = (f32[1,2048]{1,0:T(1,128)S(1)}, f32[1,2048]{1,0:T(1,128)}, u32[]{:S(2)}) copy-start(f32[1,2048]{1,0:T(1,128)} %get-tuple-element.11) | copy-start | bytes 24580
  98.4 1.9 %copy-start.25 = (f32[2048]{0:T(1024)S(1)}, f32[2048]{0:T(1024)}, u32[]{:S(2)}) copy-start(f32[2048]{0:T(1024)} %mul.227) | copy-start | bytes 24580
  119.1 1.3 copy-start.2
  122.0 4.6 %copy-start.44 = (s32[4,24]{1,0:T(4,128)S(1)}, s32[4,24]{1,0:T(4,128)}, u32[]{:S(2)}) copy-start(s32[4,24]{1,0:T(4,128)} %param.28) | copy-start | bytes 1156
  122.0 4.6 %copy-start.45 = (s32[4,24]{1,0:T(4,128)S(1)}, s32[4,24]{1,0:T(4,128)}, u32[]{:S(2)}) copy-start(s32[4,24]{1,0:T(4,128)} %param.27) | copy-start | bytes 1156
  122.0 4.6 %copy-start.49 = (s32[4]{0:T(128)S(1)}, s32[4]{0:T(128)}, u32[]{:S(2)}) copy-start(s32[4]{0:T(128)} %param.29) | copy-start | bytes 52
  122.0 45.0 %all-to-all-start.1 = ((bf16[4,512,256]{2,1,0:T(8,128)(2,1)}), bf16[4,512,256]{2,1,0:T(8,128)(2,1)}, u32[]{:S(2)}, u32[]{:S(2)}) async-start(bf16[4,512,256]{2,1,0:T(8,128)(2,1)} %copy-done.3), calls=%async_computation.1 | async-start | bytes 2097152 | tf_op jit(solution)/shard_map/all_to_all | solution.py:319
  130.5 2.9 %copy-start.43 = (bf16[2048]{0:T(1024)(128)(2,1)S(1)}, bf16[2048]{0:T(1024)(128)(2,1)}, u32[]{:S(2)}) copy-start(bf16[2048]{0:T(1024)(128)(2,1)} %param.45) | copy-start | bytes 12292
  134.1 1.2 copy-start.4
  (5 other events, 5.6 us)
Sparse Core Ops, SparseCore 0:
  13.9 105.1 all-gather.1

commit v2 on v1

--- a/solution.py
+++ b/solution.py
@@ -113,11 +113,12 @@
     )(c_rows, state, near, decay, gate_rows, norm_gain.reshape(1, -1), after)
 
 
-def choose_kernel(owner_ref, piece_ref, pool_ref, near_ref, out_ref):
+def choose_kernel(owner_ref, piece_ref, *refs):
+    out_ref = refs[-1]
     out_ref[...] = piece_ref[...]
 
 
-def choose_pieces(state_owner, spread, piece_rows, pool, near):
+def choose_pieces(state_owner, spread, piece_rows, *before):
     owners, _, state_dim = spread.shape
     block = (1, piece_rows, state_dim)
     return pl.pallas_call(
@@ -127,14 +128,13 @@
             grid=(owners,),
             in_specs=[
                 pl.BlockSpec(block, lambda i, owner: (owner[i], 0, 0)),
-                pl.BlockSpec(memory_space=pl.ANY),
-                pl.BlockSpec(memory_space=pl.ANY),
-            ],
+            ]
+            + [pl.BlockSpec(memory_space=pl.ANY)] * len(before),
             out_specs=pl.BlockSpec(block, lambda i, owner: (i, 0, 0)),
         ),
         out_shape=jax.ShapeDtypeStruct((owners, piece_rows, state_dim), BF16),
         compiler_params=pltpu.CompilerParams(vmem_limit_bytes=VMEM_LIMIT),
-    )(state_owner, spread, pool, near)
+    )(state_owner, spread, *before)
 
 
 def attend_kernel(
@@ -315,15 +315,14 @@
         conv_x, conv_b, conv_c, dt_raw[0], dt_bias, ssm_rate, skip_gain, state_dim
     )
 
-    chosen = choose_pieces(state_owner, spread, piece_rows, pool, near)
-    state = lax.all_to_all(chosen, "req", split_axis=0, concat_axis=0, tiled=True)
-    state = state.reshape(-1, state_dim)
-
     live = lax.dynamic_slice_in_dim(prefix_blocks, my_index, 1, 0)
     table = block_owner * held + block_index
     my_table = lax.dynamic_index_in_dim(table, my_index, 0, keepdims=False)
     rows = jnp.where(jnp.arange(my_table.shape[0]) < live, my_table, my_table[0])
     new_rows = kv_new[0].transpose(1, 2, 0, 3)
+    chosen = choose_pieces(state_owner, spread, piece_rows, pool, near, decay, new_rows, rows)
+    state = lax.all_to_all(chosen, "req", split_axis=0, concat_axis=0, tiled=True)
+    state = state.reshape(-1, state_dim)
     attended = attend(queries[0], new_rows, pool, rows, live, chosen)
 
     ssm_rows = ssm_tail(conv_c, state, near, decay, z_in[0], norm_gain, attended)

time: 181 us -> 174 us (0.961)
  waiting for transfers between devices: 62.4 us -> 58.6 us
  local copies, waits for them, and re-layouts: 32.6 us -> 30.6 us
    all_to_all x1, waiting for transfers between devices: 49.3 us -> 43.5 us  [body(): lax.all_to_all(outgoing, 'req', split_axis=0, concat_axis=0, tiled=True)]
    all_gather x1, waiting for transfers between devices: 13.1 us -> 15.1 us  [body(): pool = lax.all_gather(own_blocks, 'req', axis=0, tiled=True)]
    unnamed x102 -> x106, local copies, waits for them, and re-layouts: 13.4 us -> 13.5 us
  transfers between devices with their start and end apart: 3 -> 3, of which waited for: 2 -> 2; matrix products, arithmetic and copies ran while one was open for 22% -> 20% of each run, Pallas kernels for 16% -> 17%
where the time goes in v2:
time: 174 us; the launch traced here: 173 us
  waiting for transfers between devices  58.6 us (34%)
  Pallas kernels  33.5 us (19%)
  local copies, waits for them, and re-layouts  30.6 us (18%)
  other arithmetic  18.6 us (11%)
  between operations  16.6 us (10%)
  starting transfers between devices  10.9 us (6%)
  matrix products  4.22 us (2%)
    all_to_all x1, waiting for transfers between devices, body(): lax.all_to_all(outgoing, 'req', split_axis=0, concat_axis=0, tiled=True)  43.5 us
    pallas_call x1, Pallas kernels, attend(): pl.pallas_call(attend_kernel, grid_spec=pltpu.PrefetchScalarGridSpec(num_...  29.3 us
    all_gather x1, waiting for transfers between devices, body(): pool = lax.all_gather(own_blocks, 'req', axis=0, tiled=True)  15.1 us
    unnamed x106, local copies, waits for them, and re-layouts  13.5 us
    all_to_all x1, starting transfers between devices, body(): lax.all_to_all(outgoing, 'req', split_axis=0, concat_axis=0, tiled=True)  6.32 us
    add x1, other arithmetic, ssm_before_state(): intra_term + jnp.repeat(skip_gain, head_dim)[None, :] * conv_x.astype(F32)  5.77 us
    all_to_all x1, starting transfers between devices, body(): lax.all_to_all(chosen, 'req', split_axis=0, concat_axis=0, tiled=True)  4.56 us
    pallas_call x1, Pallas kernels, ssm_tail(): pl.pallas_call(tail_kernel, grid=(groups,), out_shape=jax.ShapeDtypeStruc...  3.58 us
  transfers between devices with their start and end apart: 3, of which 2 were waited for; matrix products, arithmetic and copies ran while one was open for 20% of the time, Pallas kernels for 17%

profile of v2, /device:TPU:0, one launch (start us, length us, event | category | flops | bytes accessed | tf_op | source)
XLA Modules:
  0.0 173.1 jit_solution(5746761907777572778)
XLA Ops:
  7.2 1.2 copy-done
  8.4 1.9 %convolution_bitcast_fusion = f32[4096,128]{0,1:T(8,128)} fusion(bf16[4096,128]{1,0:T(8,128)(2,1)S(1)} %bitcast.79), kind=kOutput, calls=%fused_computation.1 | convolution fusion | flops 134791168 | bytes 3145728 | tf_op jit(solution)/shard_map/dot_general | solution.py:27
  10.3 1.9 %copy.56 = f32[4096,128]{1,0:T(8,128)S(1)} copy(f32[4096,128]{0,1:T(8,128)} %convolution_bitcast_fusion) | data formatting | bytes 4194304 | tf_op jit(solution)/shard_map/reshape | solution.py:30
  12.3 1.5 multiply_convert_fusion.4
  13.9 1.7 %convert_element_type.160 = bf16[1,32,64,256]{3,2,1,0:T(8,128)(2,1)S(1)} convert(f32[1,32,64,256]{3,2,1,0:T(8,128)} %param.31) | non-fusion elementwise | flops 524288 | bytes 3145728 | tf_op jit(solution)/shard_map/convert_element_type | solution.py:287
  15.8 1.1 pad_maximum_fusion
  16.8 6.3 %all-to-all-start = ((bf16[4,560,256]{2,1,0:T(8,128)(2,1)}), bf16[4,560,256]{2,1,0:T(8,128)(2,1)S(1)}, u32[]{:S(2)}, u32[]{:S(2)}) async-start(bf16[4,560,256]{2,1,0:T(8,128)(2,1)} %pad_maximum_fusion), calls=%async_computation | async-start | bytes 2293760 | tf_op jit(solution)/shard_map/all_to_all | solution.py:298
  23.2 0.6 dynamic_slice.14
  25.3 0.6 reduce-window.6
  26.2 0.6 reduce_window_sum.25
  26.9 0.7 mul.227
  27.6 0.6 dynamic_slice.16.live_ref
  28.2 1.5 broadcast_in_dim.86
  29.8 3.1 %copy.54.refs_2_.decay_ref = f32[256,2048]{1,0:T(8,128)} copy(f32[256,2048]{0,1:T(8,128)} %bitcast.87) | data formatting | bytes 4194304 | tf_op jit(solution)/shard_map/reshape | solution.py:70
  32.8 0.8 copy.80
  34.3 0.6 iota_compare_fusion
  34.9 0.6 compare_select_fusion.2.refs_4_.rows_ref
  35.6 0.5 slice_convert_fusion.8
  36.1 0.6 slice_convert_fusion.7
  36.8 0.7 compare_select_fusion.1
  37.5 0.7 fusion.49
  38.2 0.8 copy_bitcast_fusion
  39.0 0.6 slice_convert_fusion.3
  39.6 43.5 %all-to-all-done.piece_ref = bf16[4,560,256]{2,1,0:T(8,128)(2,1)S(1)} async-done(((bf16[4,560,256]{2,1,0:T(8,128)(2,1)}), bf16[4,560,256]{2,1,0:T(8,128)(2,1)S(1)}, u32[]{:S(2)}, u32[]{:S(2)}) %all-to-all-start) | async-done | bytes 1146912 | tf_op jit(solution)/shard_map/all_to_all | solution.py:298
  83.2 0.7 constant_dynamic-slice_fusion
  83.8 0.7 reshape.206
  84.9 1.4 copy-done.11
  86.3 2.7 %fusion.11 = f32[256,2048]{1,0:T(8,128)} fusion(f32[259,2048]{1,0:T(8,128)S(1)} %maximum_convert_fusion, f32[2048]{0:T(1024)S(1)} %bitcast.100, f32[2048]{0:T(1024)S(1)} %bitcast.102, f32[2048]{0:T(1024)S(1)} %bitcast.98, f32[2048]{0:T(1024)S(1)} %bitcast.96, f32[2048]{0:T(1024)S(1)} %convert_element_type.173), kind=kLoop, calls=%fused_computation.23 | loop fusion | flops 7340032 | bytes 10526720 | tf_op jit(solution)/shard_map/convert_element_type | solution.py:61
  89.1 2.9 %copy.45 = f32[256,2048]{0,1:T(8,128)} copy(f32[256,2048]{1,0:T(8,128)} %fusion.11) | data formatting | bytes 4194304 | tf_op jit(solution)/shard_map/convert_element_type | solution.py:61
  92.3 0.3 multiply_convert_fusion.7.c_ref
  92.7 0.3 multiply_convert_fusion.6
  93.3 0.9 copy-done.12
  94.2 2.1 %fusion = f32[2,16,64,256]{3,2,1,0:T(8,128)S(1)} fusion(f32[2,16,256]{2,1,0:T(8,128)S(1)} %copy-done.27, f32[2,256,256]{2,1,0:T(8,128)S(1)} %fusion.20, pred[256,256]{1,0:T(8,128)(4,1)S(1)} %copy-done.24, f32[256,2,16,64]{0,3,2,1:T(8,128)S(1)} %bitcast.89, f32[256,2,16]{0,2,1:T(8,128)S(1)} %copy-done.28), kind=kOutput, calls=%fused_computation.2 | convolution fusion | flops 277872640 | bytes 4849664 | tf_op jit(solution)/shard_map/gkts,sgkp->tgkp/dot_general | solution.py:63
  96.3 1.8 %copy.51 = f32[256,2048]{1,0:T(8,128)} copy(f32[256,2048]{0,1:T(8,128)S(1)} %bitcast.90) | data formatting | bytes 4194304 | tf_op jit(solution)/shard_map/reshape | solution.py:68
  98.2 5.8 %multiply_add_fusion.refs_1_.near_ref = f32[256,2048]{1,0:T(8,128)S(1)} fusion(f32[256,2048]{1,0:T(8,128)} %copy.51, f32[2048]{0:T(1024)S(1)} %copy-done.26, f32[259,2048]{1,0:T(8,128)} %copy-done.11, f32[2048]{0:T(1024)S(1)} %bitcast.101, f32[2048]{0:T(1024)S(1)} %bitcast.103, f32[2048]{0:T(1024)S(1)} %bitcast.99, f32[2048]{0:T(1024)S(1)} %bitcast.97, ...), kind=kLoop, calls=%fused_computation.16 | loop fusion | flops 8388608 | bytes 12632064 | tf_op jit(solution)/shard_map/add | solution.py:69
  104.0 15.1 %all-gather.2.cloned.1.call-done.refs_0_.pool_ref = bf16[32,2,2,128,128]{4,3,2,1,0:T(8,128)(2,1)} async-done(((bf16[8,2,2,128,128]{4,3,2,1,0:T(8,128)(2,1)}), bf16[32,2,2,128,128]{4,3,2,1,0:T(8,128)(2,1)}) %all-gather.2.cloned.1.call-update) | async-done | bytes 4194320 | tf_op jit(solution)/shard_map/all_gather | solution.py:276
  119.0 1.3 copy-done.2
  120.3 0.9 copy-done.7
  121.2 0.7 shard_map.230.after_ref
  122.0 1.0 copy-done.3
  122.9 4.6 %all-to-all-start.1 = ((bf16[4,512,256]{2,1,0:T(8,128)(2,1)}), bf16[4,512,256]{2,1,0:T(8,128)(2,1)}, u32[]{:S(2)}, u32[]{:S(2)}) async-start(bf16[4,512,256]{2,1,0:T(8,128)(2,1)} %copy-done.3), calls=%async_computation.1 | async-start | bytes 2097152 | tf_op jit(solution)/shard_map/all_to_all | solution.py:324
  127.5 1.3 copy-done.4
  128.8 0.9 copy-done.8
  129.7 1.2 copy-done.10
  130.9 29.3 %shard_map.231.after_ref = bf16[256,16,128]{2,1,0:T(8,128)(2,1)} custom-call(s32[24]{0:T(128)S(1)} %compare_select_fusion.2.refs_4_.rows_ref, s32[1]{0:T(128)} %dynamic_slice.16.live_ref, bf16[256,16,128]{2,1,0:T(8,128)(2,1)S(1)} %bitcast.85, bf16[2,2,256,128]{3,2,1,0:T(8,128)(2,1)S(1)} %bitcast.84, ...), custom_call_target="tpu_custom_call" | custom-call | flops 13958643712 | bytes 6291456 | tf_op jit(solution)/shard_map/pallas_call | solution.py:218
  160.2 1.2 copy-done.5
  161.4 1.2 copy-done.6
  162.7 3.6 %shard_map.232 = bf16[256,2048]{1,0:T(8,128)(2,1)} custom-call(bf16[256,512]{1,0:T(8,128)(2,1)S(1)} %multiply_convert_fusion.7.c_ref, bf16[2048,256]{1,0:T(8,128)(2,1)} %bitcast.36.state_ref, f32[256,2048]{1,0:T(8,128)S(1)} %multiply_add_fusion.refs_1_.near_ref, f32[256,2048]{1,0:T(8,128)} %copy.54.refs_2_.decay_ref, bf16[256,2048]{1,0:T(8,128)(2,1)S(1)} %bitcast.81, ...), custom_call_target="tpu_custom_call" | custom-call | flops 268435456 | bytes 7340032 | tf_op jit(solution)/shard_map/pallas_call | solution.py:93
  (123 shorter events, 1.7 us)
Async XLA Ops:
  7.2 1.2 copy-start
  7.2 111.9 %all-gather.2.cloned.1.call-start = ((), (), s32[]{:S(2)}) async-start(), calls=%async_computation.2 | async-start | bytes 5242880 | tf_op jit(solution)/shard_map/all_gather | solution.py:276
  10.3 1.9 %copy-start.32 = (bf16[8,2,2,128]{3,2,1,0:T(2,128)(2,1)S(1)}, bf16[8,2,2,128]{3,2,1,0:T(2,128)(2,1)}, u32[]{:S(2)}) copy-start(bf16[8,2,2,128]{3,2,1,0:T(2,128)(2,1)} %param.26) | copy-start | bytes 24580
  12.2 1.6 copy-start.30
  12.2 1.6 copy-start.31
  15.7 7.5 %copy-start.9 = (s32[4]{0:T(128)S(1)}, s32[4]{0:T(128)}, u32[]{:S(2)}) copy-start(s32[4]{0:T(128)} %owner_ref.1) | copy-start | bytes 52
  15.7 9.4 %copy-start.44 = (bf16[2048]{0:T(1024)(128)(2,1)S(1)}, bf16[2048]{0:T(1024)(128)(2,1)}, u32[]{:S(2)}) copy-start(bf16[2048]{0:T(1024)(128)(2,1)} %param.43) | copy-start | bytes 12292
  15.7 9.4 %copy-start.49 = (f32[32]{0:T(128)S(1)}, f32[32]{0:T(128)}, u32[]{:S(2)}) copy-start(f32[32]{0:T(128)} %param.38) | copy-start | bytes 388
  15.7 9.5 %copy-start.17 = (f32[1,256,32]{1,2,0:T(8,128)S(1)}, f32[1,256,32]{1,2,0:T(8,128)}, u32[]{:S(2)}) copy-start(f32[1,256,32]{1,2,0:T(8,128)} %param.37) | copy-start | bytes 98308
  15.7 9.4 %copy-start.48 = (f32[32]{0:T(128)S(1)}, f32[32]{0:T(128)}, u32[]{:S(2)}) copy-start(f32[32]{0:T(128)} %param.39) | copy-start | bytes 388
  15.7 11.1 %copy-start.50 = (f32[32]{0:T(128)S(1)}, f32[32]{0:T(128)}, u32[]{:S(2)}) copy-start(f32[32]{0:T(128)} %param.40) | copy-start | bytes 388
  15.8 11.8 %copy-start.51 = (s32[4]{0:T(128)S(1)}, s32[4]{0:T(128)}, u32[]{:S(2)}) copy-start(s32[4]{0:T(128)} %param.29) | copy-start | bytes 52
  16.8 66.3 %all-to-all-start = ((bf16[4,560,256]{2,1,0:T(8,128)(2,1)}), bf16[4,560,256]{2,1,0:T(8,128)(2,1)S(1)}, u32[]{:S(2)}, u32[]{:S(2)}) async-start(bf16[4,560,256]{2,1,0:T(8,128)(2,1)} %pad_maximum_fusion), calls=%async_computation | async-start | bytes 2293760 | tf_op jit(solution)/shard_map/all_to_all | solution.py:298
  29.7 3.1 %copy-start.16 = (bf16[1,256,2,2,128]{4,3,2,1,0:T(2,128)(2,1)S(1)}, bf16[1,256,2,2,128]{4,3,2,1,0:T(2,128)(2,1)}, u32[]{:S(2)}) copy-start(bf16[1,256,2,2,128]{4,3,2,1,0:T(2,128)(2,1)} %param.24) | copy-start | bytes 786436
  29.7 4.5 %copy-start.46 = (s32[4,24]{1,0:T(4,128)S(1)}, s32[4,24]{1,0:T(4,128)}, u32[]{:S(2)}) copy-start(s32[4,24]{1,0:T(4,128)} %param.28) | copy-start | bytes 1156
  29.7 4.5 %copy-start.47 = (s32[4,24]{1,0:T(4,128)S(1)}, s32[4,24]{1,0:T(4,128)}, u32[]{:S(2)}) copy-start(s32[4,24]{1,0:T(4,128)} %param.27) | copy-start | bytes 1156
  29.7 5.9 %copy-start.33 = (bf16[2,512]{1,0:T(2,128)(2,1)S(1)}, bf16[2,512]{1,0:T(2,128)(2,1)}, u32[]{:S(2)}) copy-start(bf16[2,512]{1,0:T(2,128)(2,1)} %param.44) | copy-start | bytes 6148
  29.7 6.4 %copy-start.29 = (bf16[4,2,512]{2,1,0:T(2,128)(2,1)S(1)}, bf16[4,2,512]{2,1,0:T(2,128)(2,1)}, u32[]{:S(2)}) copy-start(bf16[4,2,512]{2,1,0:T(2,128)(2,1)} %param.42) | copy-start | bytes 24580
  29.7 7.7 %copy-start.13 = (bf16[1,256,2,512]{3,2,1,0:T(2,128)(2,1)S(1)}, bf16[1,256,2,512]{3,2,1,0:T(2,128)(2,1)}, u32[]{:S(2)}) copy-start(bf16[1,256,2,512]{3,2,1,0:T(2,128)(2,1)} %param.35) | copy-start | bytes 1572868
  32.8 6.2 %copy-start.25 = (bf16[4,2048]{1,0:T(4,128)(2,1)S(1)}, bf16[4,2048]{1,0:T(4,128)(2,1)}, u32[]{:S(2)}) copy-start(bf16[4,2048]{1,0:T(4,128)(2,1)} %param.41) | copy-start | bytes 49156
  38.2 46.4 %copy-start.14 = (bf16[1,256,2048]{2,1,0:T(8,128)(2,1)S(1)}, bf16[1,256,2048]{2,1,0:T(8,128)(2,1)}, u32[]{:S(2)}) copy-start(bf16[1,256,2048]{2,1,0:T(8,128)(2,1)} %param.34) | copy-start | bytes 3145732
  83.2 5.9 %copy-start.1 = (bf16[4,560,256]{2,1,0:T(8,128)(2,1)}, bf16[4,560,256]{2,1,0:T(8,128)(2,1)S(1)}, u32[]{:S(2)}) copy-start(bf16[4,560,256]{2,1,0:T(8,128)(2,1)S(1)} %all-to-all-done.piece_ref) | copy-start | bytes 3440644
  84.6 1.7 %copy-start.18 = (f32[1,2048]{1,0:T(1,128)S(1)}, f32[1,2048]{1,0:T(1,128)}, u32[]{:S(2)}) copy-start(f32[1,2048]{1,0:T(1,128)} %get-tuple-element.9) | copy-start | bytes 24580
  84.6 1.7 %copy-start.20 = (f32[1,2048]{1,0:T(1,128)S(1)}, f32[1,2048]{1,0:T(1,128)}, u32[]{:S(2)}) copy-start(f32[1,2048]{1,0:T(1,128)} %get-tuple-element.10) | copy-start | bytes 24580
  84.6 1.7 %copy-start.22 = (f32[1,2048]{1,0:T(1,128)S(1)}, f32[1,2048]{1,0:T(1,128)}, u32[]{:S(2)}) copy-start(f32[1,2048]{1,0:T(1,128)} %get-tuple-element.11) | copy-start | bytes 24580
  84.9 1.4 copy-start.11
  89.0 3.0 %copy-start.15 = (bf16[256,512]{1,0:T(8,128)(2,1)S(1)}, bf16[256,512]{1,0:T(8,128)(2,1)}, u32[]{:S(2)}) copy-start(bf16[256,512]{1,0:T(8,128)(2,1)} %get-tuple-element.25) | copy-start | bytes 786436
  89.0 3.2 %copy-start.38 = (f32[1,1,512]{2,1,0:T(1,128)S(1)}, f32[1,1,512]{2,1,0:T(1,128)}, u32[]{:S(2)}) copy-start(f32[1,1,512]{2,1,0:T(1,128)} %get-tuple-element.14) | copy-start | bytes 6148
  89.0 3.2 %copy-start.39 = (f32[1,1,512]{2,1,0:T(1,128)S(1)}, f32[1,1,512]{2,1,0:T(1,128)}, u32[]{:S(2)}) copy-start(f32[1,1,512]{2,1,0:T(1,128)} %get-tuple-element.15) | copy-start | bytes 6148
  89.0 3.2 %copy-start.40 = (f32[1,1,512]{2,1,0:T(1,128)S(1)}, f32[1,1,512]{2,1,0:T(1,128)}, u32[]{:S(2)}) copy-start(f32[1,1,512]{2,1,0:T(1,128)} %get-tuple-element.16) | copy-start | bytes 6148
  89.0 3.2 %copy-start.41 = (f32[1,1,512]{2,1,0:T(1,128)S(1)}, f32[1,1,512]{2,1,0:T(1,128)}, u32[]{:S(2)}) copy-start(f32[1,1,512]{2,1,0:T(1,128)} %get-tuple-element.17) | copy-start | bytes 6148
  89.1 3.2 %copy-start.43 = (f32[1,512]{1,0:T(1,128)S(1)}, f32[1,512]{1,0:T(1,128)}, u32[]{:S(2)}) copy-start(f32[1,512]{1,0:T(1,128)} %get-tuple-element.23) | copy-start | bytes 6148
  92.6 1.6 copy-start.12
  92.6 1.6 copy-start.24
  92.6 1.6 copy-start.27
  92.6 1.6 copy-start.28
  96.3 1.9 %copy-start.19 = (f32[1,2048]{1,0:T(1,128)S(1)}, f32[1,2048]{1,0:T(1,128)}, u32[]{:S(2)}) copy-start(f32[1,2048]{1,0:T(1,128)} %get-tuple-element.9) | copy-start | bytes 24580
  96.3 1.9 %copy-start.21 = (f32[1,2048]{1,0:T(1,128)S(1)}, f32[1,2048]{1,0:T(1,128)}, u32[]{:S(2)}) copy-start(f32[1,2048]{1,0:T(1,128)} %get-tuple-element.10) | copy-start | bytes 24580
  96.3 1.8 %copy-start.23 = (f32[1,2048]{1,0:T(1,128)S(1)}, f32[1,2048]{1,0:T(1,128)}, u32[]{:S(2)}) copy-start(f32[1,2048]{1,0:T(1,128)} %get-tuple-element.11) | copy-start | bytes 24580
  96.3 1.8 %copy-start.26 = (f32[2048]{0:T(1024)S(1)}, f32[2048]{0:T(1024)}, u32[]{:S(2)}) copy-start(f32[2048]{0:T(1024)} %mul.227) | copy-start | bytes 24580
  119.0 1.3 copy-start.2
  121.9 1.0 copy-start.3
  122.9 4.6 %copy-start.45 = (bf16[2048]{0:T(1024)(128)(2,1)S(1)}, bf16[2048]{0:T(1024)(128)(2,1)}, u32[]{:S(2)}) copy-start(bf16[2048]{0:T(1024)(128)(2,1)} %param.45) | copy-start | bytes 12292
  122.9 37.3 %all-to-all-start.1 = ((bf16[4,512,256]{2,1,0:T(8,128)(2,1)}), bf16[4,512,256]{2,1,0:T(8,128)(2,1)}, u32[]{:S(2)}, u32[]{:S(2)}) async-start(bf16[4,512,256]{2,1,0:T(8,128)(2,1)} %copy-done.3), calls=%async_computation.1 | async-start | bytes 2097152 | tf_op jit(solution)/shard_map/all_to_all | solution.py:324
  127.5 1.3 copy-start.4
  129.7 1.2 copy-start.10
  160.2 1.2 copy-start.5
  161.4 1.2 copy-start.6
  (7 other events, 5.3 us)
Sparse Core Ops, SparseCore 0:
  13.9 105.0 all-gather.1
